TPU v7x, 32 devices: a whole 2x2x4 slice. The times are simulated.
32 devices in a mesh: groups: 2 (over y), img: 4 (over z), samp: 2 (over x), sub: 2 (over core).
Axes of the slice: x: 2, y: 2, z: 4, core: 2. Of those that a mesh axis runs over, the one named last changes fastest.
Arguments:
- images: bfloat16 [2, 4096, 16384], P(None, ('groups', 'img'), ('samp', 'sub')), parts along dimension 1, may hold values from -6 to 6
- references: bfloat16 [2, 32, 16384], P(None, 'img', ('samp', 'sub')), may hold values from -0.03125 to 0.03125
- noise_weight: float32 [16384], P(('samp', 'sub')), may hold values from 0.3 to 3
- normalizer: float32 [4096], P(('groups', 'img')), parts along dimension 0, may hold values from -1 to 1
- owner_order: int32 [32], replicated, may hold values from 0 to 31, each once
Outputs:
- weighted_sums: bfloat16 [32, 4, 16384], P('img', 'groups', ('samp', 'sub')), parts along dimension 1
There are 2 independent parts, one for each index of `groups`. A program takes and returns all parts, laid end to end along the dimension named above; an argument that names none is the same for every part. Nothing has to cross between parts.
Inputs may be any that keep to these rules, and one draw needn't show every extreme that they name: `owner_order`: each orientation appears exactly once.
All inputs are finite; a program needn't handle non-finite values.
Results may differ from a plain program's by a relative error of at most 0.012.
The roundings to bfloat16 on the way count: a program that leaves them out, or rounds other values in their place, can miss the bound.
Values may be sent and summed in bfloat16 or wider, within the bound.
A program may use at most 64 MiB of HBM per device.

v0:
```python
import jax
import jax.numpy as jnp
from jax import lax
from jax.sharding import PartitionSpec as P


def local(images, references, noise_weight, normalizer, owner_order):
    refs = lax.all_gather(references, "img", axis=1, tiled=True).astype(jnp.float32)
    scaled = refs * noise_weight[None, None, :]
    weighted_refs = scaled.astype(jnp.bfloat16)
    half_power = 0.5 * jnp.sum(refs * scaled, axis=(0, 2))
    cross = lax.dot_general(
        images, weighted_refs, (((0, 2), (0, 2)), ((), ())), preferred_element_type=jnp.float32
    )
    partial_scores = cross - half_power[None, :]
    total = lax.psum(partial_scores, ("samp", "sub"))
    posterior = jnp.exp(total - normalizer[:, None]).astype(jnp.bfloat16)
    groups_img = lax.axis_size("img")
    scale_factor = 1.0 / jnp.sqrt(jnp.float32(images.shape[1] * groups_img))
    local_sums = lax.dot_general(
        posterior, images, (((0,), (1,)), ((), ())), preferred_element_type=jnp.float32
    )
    ordered = jnp.take(local_sums, owner_order, axis=0)
    result = lax.psum_scatter(ordered, "img", scatter_dimension=0, tiled=True)
    return (result * scale_factor).astype(jnp.bfloat16)


def solution(mesh):
    in_specs = (
        P(None, ("groups", "img"), ("samp", "sub")),
        P(None, "img", ("samp", "sub")),
        P(("samp", "sub")),
        P(("groups", "img")),
        P(),
    )
    out_specs = P("img", "groups", ("samp", "sub"))
    return jax.shard_map(local, mesh=mesh, in_specs=in_specs, out_specs=out_specs, check_vma=False)
```

profile of v0, /device:TPU:0, one launch (start us, length us, event | category | flops | bytes accessed | tf_op | source)
XLA Modules:
  0.0 134.5 jit_solution(4648390263706312099)
XLA Ops:
  6.5 0.0 copy-start.1
  6.5 0.0 copy-start
  6.5 0.0 all-reduce.4.cloned.1.call-start
  6.5 17.7 %all_gather.3 = bf16[2,32,4096]{2,1,0:T(8,128)(2,1)S(1)} all-gather(bf16[2,8,4096]{2,1,0:T(8,128)(2,1)} %param.6), channel_id=1, replica_groups=mesh['groups'=2,'img'=4,'samp'=2,'sub'=2] {'img'}, dimensions={1}, use_global_device_ids=true | all-gather | bytes 655360 | tf_op jit(solution)/shard_map/all_gather | solution.py:8
  24.2 1.0 fusion.2
  25.2 6.6 %fusion.1 = f32[512,32]{0,1:T(8,128)} fusion(bf16[2,512,4096]{2,1,0:T(8,128)(2,1)} %param.5, bf16[2,32,4096]{2,1,0:T(8,128)(2,1)S(1)} %all_gather.3, f32[4096]{0:T(1024)} %param.7, f32[32]{0:T(128)S(1)} %broadcast_multiply_fusion), kind=kOutput, calls=%fused_computation.5 | convolution fusion | flops 269238272 | bytes 8994944 | tf_op jit(solution)/shard_map/dot_general | solution.py:12
  31.8 0.0 all-reduce.4.cloned.1.call-update
  31.8 0.0 all-reduce.6.cloned.1.call-start
  31.9 0.0 copy-done.1
  31.9 0.0 copy-start.2
  32.0 32.8 %all-reduce.4.cloned.1.call-done = f32[512,32]{0,1:T(8,128)} async-done(((f32[512,32]{0,1:T(8,128)}), f32[512,32]{0,1:T(8,128)}) %all-reduce.4.cloned.1.call-update) | async-done | bytes 65552 | tf_op jit(solution)/shard_map/psum | solution.py:16
  64.8 0.0 copy-done
  64.8 4.9 %fusion.6 = f32[32,2,4096]{2,0,1:T(8,128)S(1)} fusion(bf16[2,512,4096]{2,1,0:T(8,128)(2,1)} %param.5, f32[512,32]{0,1:T(8,128)} %all-reduce.4.cloned.1.call-done, f32[512]{0:T(512)S(1)} %copy-done), kind=kOutput, calls=%fused_computation.13 | convolution fusion | flops 268468224 | bytes 9504768 | tf_op jit(solution)/shard_map/dot_general | solution.py:20
  69.7 0.8 copy.8
  70.6 1.7 %gather_fusion = f32[32,2,4096]{2,1,0:T(2,128)S(1)} fusion(f32[32,2,4096]{2,1,0:T(2,128)S(1)} %copy.8, s32[1024]{0:T(1024)S(1)} %pad_clamp_fusion), kind=kCustom, calls=%fused_computation | custom fusion | bytes 2097280 | tf_op jit(solution)/shard_map/jit(_take)/gather | solution.py:23
  72.2 1.6 %broadcast_select_fusion = f32[32,2,4096]{2,1,0:T(2,128)} fusion(f32[32,2,4096]{2,1,0:T(2,128)S(1)} %gather_fusion, pred[32]{0:T(512)(128)(4,1)S(1)} %compare_and_fusion), kind=kLoop, calls=%fused_computation.7 | loop fusion | flops 262144 | bytes 2097184 | tf_op jit(solution)/shard_map/jit(_take)/select_n | solution.py:23
  73.9 0.0 all-reduce.6.cloned.1.call-update
  73.9 0.0 copy-done.2
  73.9 0.6 dynamic-slice
  75.2 50.7 %all-reduce.6.cloned.1.call-done = f32[32,2,4096]{2,1,0:T(2,128)} async-done(((f32[32,2,4096]{2,1,0:T(2,128)}), f32[32,2,4096]{2,1,0:T(2,128)}) %all-reduce.6.cloned.1.call-update) | async-done | bytes 1048592
  125.9 1.7 %fusion.4 = bf16[8,2,4096]{2,1,0:T(2,128)(2,1)} fusion(f32[32,2,4096]{2,1,0:T(2,128)} %all-reduce.6.cloned.1.call-done, u32[]{:T(128)S(6)} %multiply.1), kind=kLoop, calls=%fused_computation.10 | loop fusion | flops 131072 | bytes 393220 | tf_op jit(solution)/shard_map/convert_element_type | solution.py:25
  (4 shorter events, 0.0 us)
Async XLA Ops:
  6.5 25.4 %copy-start.1 = (s32[32]{0:T(128)S(1)}, s32[32]{0:T(128)}, u32[]{:S(2)}) copy-start(s32[32]{0:T(128)} %param.9) | copy-start | bytes 388
  6.5 58.3 %copy-start = (f32[512]{0:T(512)S(1)}, f32[512]{0:T(512)}, u32[]{:S(2)}) copy-start(f32[512]{0:T(512)} %param.8) | copy-start | bytes 6148
  6.5 58.3 %all-reduce.4.cloned.1.call-start = ((), (), s32[]{:S(2)}) async-start(), calls=%async_computation | async-start | bytes 131072 | tf_op jit(solution)/shard_map/psum | solution.py:16
  31.8 94.0 %all-reduce.6.cloned.1.call-start = ((), (), s32[]{:S(2)}) async-start(), calls=%async_computation.1 | async-start | bytes 2097152
  31.9 42.0 %copy-start.2 = (u32[32]{0:T(128)S(1)}, u32[32]{0:T(128)}, u32[]{:S(2)}) copy-start(u32[32]{0:T(128)} %constant.24) | copy-start | bytes 388
Sparse Core Ops, SparseCore 0:
  32.0 32.7 all-reduce.3
  74.0 51.8 all-reduce.5
where the time goes:
time: 135 us; the launch traced here: 134 us
  waiting for transfers between devices  83.6 us (62%)
  blocking collectives  17.7 us (13%)
  between operations  14.1 us (10%)
  matrix products  11.6 us (9%)
  other arithmetic  4.36 us (3%)
  local copies, waits for them, and re-layouts  3.08 us (2%)
    unnamed x3, waiting for transfers between devices  50.8 us
    psum x1, waiting for transfers between devices, local(): total = lax.psum(partial_scores, ('samp', 'sub'))  32.8 us
    all_gather x1, blocking collectives, local(): lax.all_gather(references, 'img', axis=1, tiled=True).astype(jnp.float32)  17.7 us
    dot_general x1, matrix products, local(): lax.dot_general(images, weighted_refs, (((0, 2), (0, 2)), ((), ())), pref...  6.62 us
    dot_general x1, matrix products, local(): lax.dot_general(posterior, images, (((0,), (1,)), ((), ())), preferred_el...  4.94 us
  transfers between devices with their start and end apart: 2, of which 2 were waited for; matrix products, arithmetic and copies ran while one was open for 0% of the time, Pallas kernels for 0%

commit v1 on v0

v1 whole, which is shorter than its diff:
```python
import functools

import jax
import jax.numpy as jnp
from jax import lax
from jax.experimental import pallas as pl
from jax.experimental.pallas import tpu as pltpu
from jax.sharding import PartitionSpec as P

MESH = pl.DeviceIdType.MESH
F32, BF16 = jnp.float32, jnp.bfloat16


def kernel(n, nx, nc, scale, refs_hbm, images_hbm, noise, norm, order, out,
           img_v, gat, sc_send, sc_recv, post, sbuf, rbuf, own,
           img_sem, own_sem, g_send, g_recv, s_send, s_recv, p_send, p_recv, o_send, o_recv):
    ns = 2 * nx
    rows = refs_hbm.shape[1]
    orient = n * rows
    count = images_hbm.shape[1]
    ch = images_hbm.shape[2] // nc
    me = lax.axis_index("img")
    mx = lax.axis_index("samp")
    mc = lax.axis_index("sub")
    ms = mx * 2 + mc

    def cols(c):
        return pl.ds(pl.multiple_of(c * ch, ch), ch)

    def img_peer(r):
        return lax.rem(me + r, n)

    def samp_peer(r):
        t = lax.rem(ms + r, ns)
        return t, {"samp": t // 2, "sub": lax.rem(t, 2)}

    def image_copy(c, p):
        return pltpu.make_async_copy(images_hbm.at[p, :, cols(c)], img_v.at[c, p], img_sem.at[c, p])

    def own_copy(c):
        return pltpu.make_async_copy(refs_hbm.at[:, :, cols(c)], gat.at[c, me], own_sem.at[c])

    def gather_copy(c, r, slot):
        return pltpu.make_async_remote_copy(
            refs_hbm.at[:, :, cols(c)], gat.at[c, slot], g_send.at[c, r - 1], g_recv.at[c, r - 1],
            device_id={"img": img_peer(r)}, device_id_type=MESH)

    def score_copy(r):
        t, dev = samp_peer(r)
        return pltpu.make_async_remote_copy(
            sc_send.at[t], sc_recv.at[r - 1], s_send.at[r - 1], s_recv.at[r - 1],
            device_id=dev, device_id_type=MESH)

    def post_copy(r, slot):
        _, dev = samp_peer(r)
        return pltpu.make_async_remote_copy(
            post.at[slot], post.at[slot], p_send.at[r - 1], p_recv.at[r - 1],
            device_id=dev, device_id_type=MESH)

    def sum_copy(c, r):
        d = img_peer(r)
        return pltpu.make_async_remote_copy(
            sbuf.at[c, d], rbuf.at[c, r - 1], o_send.at[c, r - 1], o_recv.at[c, r - 1],
            device_id={"img": d}, device_id_type=MESH)

    barrier = pltpu.get_barrier_semaphore()
    for r in range(1, n):
        pl.semaphore_signal(barrier, inc=1, device_id={"img": img_peer(r)}, device_id_type=MESH)
    for r in range(1, ns):
        pl.semaphore_signal(barrier, inc=1, device_id=samp_peer(r)[1], device_id_type=MESH)
    for c in range(nc):
        own_copy(c).start()
        for p in range(2):
            image_copy(c, p).start()
    pl.semaphore_wait(barrier, n - 1 + ns - 1)
    for c in range(nc):
        for r in range(1, n):
            gather_copy(c, r, me).start()

    perm = (lax.broadcasted_iota(jnp.int32, (orient, orient), 1) == order[...]).astype(F32).astype(BF16)

    def score_step(c, carry):
        total, power = carry
        own_copy(c).wait()
        for p in range(2):
            image_copy(c, p).wait()
        for r in range(1, n):
            gather_copy(c, r, lax.rem(me + n - r, n)).wait_recv()
        weight = noise[:, cols(c)]
        for p in range(2):
            block = gat[c, :, p].astype(F32).reshape(orient, ch).astype(BF16)
            refs = jnp.dot(perm, block, preferred_element_type=F32)
            scaled = refs * weight
            power = power + jnp.sum(refs * scaled, axis=1, keepdims=True)
            total = total + lax.dot_general(
                scaled.astype(BF16), img_v[c, p], (((1,), (1,)), ((), ())), preferred_element_type=F32)
        return total, power

    total, power = lax.fori_loop(
        0, nc, score_step, (jnp.zeros((orient, count), F32), jnp.zeros((orient, 1), F32)))
    sc_send[...] = (total - 0.5 * power).reshape(sc_send.shape)
    for r in range(1, ns):
        score_copy(r).start()
    score = sc_send[ms]
    for r in range(1, ns):
        score_copy(r).wait_recv()
        score = score + sc_recv[r - 1]
    post[ms] = jnp.exp(score - norm[...]).astype(BF16)
    for r in range(1, ns):
        post_copy(r, ms).start()
    for r in range(1, ns):
        post_copy(r, lax.rem(ms + ns - r, ns)).wait_recv()
    weights = post[...].astype(F32).reshape(orient, count).astype(BF16)

    def sum_step(c, _):
        for p in range(2):
            sums = jnp.dot(weights, img_v[c, p], preferred_element_type=F32).reshape(n, rows, ch)
            own[c, :, p] = sums
            sbuf[c, :, p] = sums.astype(BF16)
        for r in range(1, n):
            sum_copy(c, r).start()
        return 0

    lax.fori_loop(0, nc, sum_step, 0)

    def out_step(c, _):
        value = own[c, me]
        for r in range(1, n):
            sum_copy(c, r).wait_recv()
            value = value + rbuf[c, r - 1].astype(F32)
        out[:, :, cols(c)] = (value * scale).astype(BF16)
        return 0

    lax.fori_loop(0, nc, out_step, 0)

    for r in range(1, ns):
        score_copy(r).wait_send()
        post_copy(r, ms).wait_send()

    def drain(c, _):
        for r in range(1, n):
            gather_copy(c, r, me).wait_send()
            sum_copy(c, r).wait_send()
        return 0

    lax.fori_loop(0, nc, drain, 0)


def local(images, references, noise_weight, normalizer, owner_order, *, n, nx):
    ns = 2 * nx
    _, rows, samples = references.shape
    count = images.shape[1]
    orient = n * rows
    ch = 1024
    nc = samples // ch
    scale = 1.0 / (float(count * n) ** 0.5)
    dma = pltpu.SemaphoreType.DMA
    vmem = pl.BlockSpec(memory_space=pltpu.VMEM)
    hbm = pl.BlockSpec(memory_space=pl.ANY)
    out = pl.pallas_call(
        functools.partial(kernel, n, nx, nc, scale),
        out_shape=jax.ShapeDtypeStruct((2, rows, samples), BF16),
        in_specs=[hbm, hbm, vmem, vmem, vmem],
        out_specs=vmem,
        scratch_shapes=[
            pltpu.VMEM((nc, 2, count, ch), BF16),
            pltpu.VMEM((nc, n, 2, rows, ch), BF16),
            pltpu.VMEM((ns, orient // ns, count), F32),
            pltpu.VMEM((ns - 1, orient // ns, count), F32),
            pltpu.VMEM((ns, orient // ns, count), BF16),
            pltpu.VMEM((nc, n, 2, rows, ch), BF16),
            pltpu.VMEM((nc, n - 1, 2, rows, ch), BF16),
            pltpu.VMEM((nc, n, 2, rows, ch), F32),
            dma((nc, 2)),
            dma((nc,)),
            dma((nc, n - 1)),
            dma((nc, n - 1)),
            dma((ns - 1,)),
            dma((ns - 1,)),
            dma((ns - 1,)),
            dma((ns - 1,)),
            dma((nc, n - 1)),
            dma((nc, n - 1)),
        ],
        compiler_params=pltpu.CompilerParams(
            collective_id=0, has_side_effects=True, vmem_limit_bytes=48 * 1024 * 1024),
        cost_estimate=pl.CostEstimate(
            flops=8 * orient * count * samples, bytes_accessed=4 * count * samples,
            transcendentals=orient * count),
    )(references, images, noise_weight.reshape(1, samples), normalizer.reshape(1, count),
      owner_order.reshape(orient, 1))
    return jnp.transpose(out, (1, 0, 2))


def solution(mesh):
    in_specs = (
        P(None, ("groups", "img"), ("samp", "sub")),
        P(None, "img", ("samp", "sub")),
        P(("samp", "sub")),
        P(("groups", "img")),
        P(),
    )
    out_specs = P("img", "groups", ("samp", "sub"))
    body = functools.partial(local, n=mesh.shape["img"], nx=mesh.shape["samp"])
    return jax.shard_map(body, mesh=mesh, in_specs=in_specs, out_specs=out_specs, check_vma=False)
```

time: 135 us -> 41.9 us (0.31)
  waiting for transfers between devices: 83.6 us -> 0 us
  Pallas kernels: 0 us -> 37.8 us
  blocking collectives: 17.7 us -> 0 us
  between operations: 14.1 us -> 0.01 us
  matrix products: 11.6 us -> 0 us
  other arithmetic: 4.36 us -> 0 us
    unnamed x3 -> x0, waiting for transfers between devices: 50.8 us -> none
    pallas_call x0 -> x1, Pallas kernels: none -> 37.8 us  [local(): pl.pallas_call(functools.partial(kernel, n, nx, nc, scale), out_shape=jax...]
    psum x1 -> x0, waiting for transfers between devices: 32.8 us -> none  [local(): total = lax.psum(partial_scores, ('samp', 'sub'))]
    all_gather x1 -> x0, blocking collectives: 17.7 us -> none  [local(): lax.all_gather(references, 'img', axis=1, tiled=True).astype(jnp.float32)]
    dot_general x2 -> x0, matrix products: 11.6 us -> none  [the longest x1 6.62 us: local(): lax.dot_general(images, weighted_refs, (((0, 2), (0, 2)), ((), ())), pref...]
    convert_element_type x1 -> x0, other arithmetic: 1.74 us -> none  [local(): return (result * scale_factor).astype(jnp.bfloat16)]
    unnamed x7 -> x6, local copies, waits for them, and re-layouts: 0.6 us -> 2.3 us
    gather x1 -> x0, local copies, waits for them, and re-layouts: 1.67 us -> none  [local(): ordered = jnp.take(local_sums, owner_order, axis=0)]
  transfers between devices with their start and end apart: 2 -> 0, of which waited for: 2 -> 0; matrix products, arithmetic and copies ran while one was open for 0% -> 0% of each run, Pallas kernels for 0% -> 0%
where the time goes in v1:
time: 41.9 us; the launch traced here: 41.6 us
  Pallas kernels  37.8 us (90%)
  local copies, waits for them, and re-layouts  3.83 us (9%)
    pallas_call x1, Pallas kernels, local(): pl.pallas_call(functools.partial(kernel, n, nx, nc, scale), out_shape=jax...  37.8 us
    unnamed x6, local copies, waits for them, and re-layouts  2.3 us

profile of v1, /device:TPU:0, one launch (start us, length us, event | category | flops | bytes accessed | tf_op | source)
XLA Modules:
  0.0 41.6 jit_solution(17181296955335120563)
XLA Ops:
  0.0 0.7 %copy.6.order = s32[32,1]{1,0:T(8,128)S(1)} copy(s32[32,1]{0,1:T(1,128)} %bitcast.7) | data formatting | bytes 256 | tf_op jit(solution)/shard_map/reshape | solution.py:191
  0.7 0.0 copy-start
  0.7 0.9 %copy-done = bf16[2,8,4096]{2,1,0:T(8,128)(2,1)S(1)} copy-done((bf16[2,8,4096]{2,1,0:T(8,128)(2,1)S(1)}, bf16[2,8,4096]{2,1,0:T(8,128)(2,1)}, u32[]{:S(2)}) %copy-start) | copy-done | bytes 131096
  1.6 0.0 copy-start.1
  1.6 0.7 %copy-done.1 = f32[4096]{0:T(1024)S(1)} copy-done((f32[4096]{0:T(1024)S(1)}, f32[4096]{0:T(1024)}, u32[]{:S(2)}) %copy-start.1) | copy-done | bytes 16408
  2.4 0.0 copy-start.2
  2.4 0.7 %copy-done.2 = f32[512]{0:T(512)S(1)} copy-done((f32[512]{0:T(512)S(1)}, f32[512]{0:T(512)}, u32[]{:S(2)}) %copy-start.2) | copy-done | bytes 2072
  3.0 37.8 %shard_map.55 = bf16[2,8,4096]{2,1,0:T(8,128)(2,1)S(1)} custom-call(bf16[2,8,4096]{2,1,0:T(8,128)(2,1)S(1)} %copy-done, bf16[2,512,4096]{2,1,0:T(8,128)(2,1)} %images_hbm.1, f32[1,4096]{1,0:T(1,128)S(1)} %bitcast.5, f32[1,512]{1,0:T(1,128)S(1)} %bitcast.6, s32[32,1]{1,0:T(8,128)S(1)} %copy.6.order), custom_call_target="tpu_custom_call" | custom-call | flops 536870912 | bytes 8388608 | tf_op jit(solution)/shard_map/pallas_call | solution.py:160
  40.8 0.8 %copy.7 = bf16[8,2,4096]{2,1,0:T(2,128)(2,1)} copy(bf16[8,2,4096]{2,0,1:T(8,128)(2,1)S(1)} %bitcast.4) | data formatting | bytes 262144 | tf_op jit(solution)/shard_map/transpose | solution.py:192
Async XLA Ops:
  0.7 0.9 %copy-start = (bf16[2,8,4096]{2,1,0:T(8,128)(2,1)S(1)}, bf16[2,8,4096]{2,1,0:T(8,128)(2,1)}, u32[]{:S(2)}) copy-start(bf16[2,8,4096]{2,1,0:T(8,128)(2,1)} %refs_hbm.1) | copy-start | bytes 393220
  1.6 0.7 %copy-start.1 = (f32[4096]{0:T(1024)S(1)}, f32[4096]{0:T(1024)}, u32[]{:S(2)}) copy-start(f32[4096]{0:T(1024)} %param.7) | copy-start | bytes 49156
  2.4 0.7 %copy-start.2 = (f32[512]{0:T(512)S(1)}, f32[512]{0:T(512)}, u32[]{:S(2)}) copy-start(f32[512]{0:T(512)} %param.8) | copy-start | bytes 6148

commit v2 on v1

--- a/solution.py
+++ b/solution.py
@@ -11,15 +11,16 @@
 F32, BF16 = jnp.float32, jnp.bfloat16
 
 
-def kernel(n, nx, nc, scale, refs_hbm, images_hbm, noise, norm, order, out,
-           img_v, gat, sc_send, sc_recv, post, sbuf, rbuf, own,
-           img_sem, own_sem, g_send, g_recv, s_send, s_recv, p_send, p_recv, o_send, o_recv):
+def kernel(n, nx, nc, scale, refs_hbm, images_hbm, noise_hbm, norm_hbm, order_hbm, out,
+           noise, norm, order, img_v, gat, sc_send, sc_recv, post, sbuf, rbuf, own,
+           small_sem, img_sem, own_sem, g_send, g_recv, f_send, f_recv, s_send, s_recv, p_send, p_recv, o_send, o_recv):
     ns = 2 * nx
     rows = refs_hbm.shape[1]
     orient = n * rows
     count = images_hbm.shape[1]
     ch = images_hbm.shape[2] // nc
     me = lax.axis_index("img")
+    mg = lax.axis_index("groups")
     mx = lax.axis_index("samp")
     mc = lax.axis_index("sub")
     ms = mx * 2 + mc
@@ -38,12 +39,18 @@
         return pltpu.make_async_copy(images_hbm.at[p, :, cols(c)], img_v.at[c, p], img_sem.at[c, p])
 
     def own_copy(c):
-        return pltpu.make_async_copy(refs_hbm.at[:, :, cols(c)], gat.at[c, me], own_sem.at[c])
+        return pltpu.make_async_copy(refs_hbm.at[:, :, cols(c)], gat.at[c, :, me], own_sem.at[c])
 
     def gather_copy(c, r, slot):
         return pltpu.make_async_remote_copy(
-            refs_hbm.at[:, :, cols(c)], gat.at[c, slot], g_send.at[c, r - 1], g_recv.at[c, r - 1],
+            refs_hbm.at[mg, :, cols(c)], gat.at[c, mg, slot], g_send.at[c, r - 1], g_recv.at[c, r - 1],
             device_id={"img": img_peer(r)}, device_id_type=MESH)
+
+    def forward_copy(c, r, part):
+        block = gat.at[c, part, lax.rem(me + n - r, n)]
+        return pltpu.make_async_remote_copy(
+            block, block, f_send.at[c, r - 1], f_recv.at[c, r - 1],
+            device_id={"groups": 1 - mg}, device_id_type=MESH)
 
     def score_copy(r):
         t, dev = samp_peer(r)
@@ -64,31 +71,51 @@
             device_id={"img": d}, device_id_type=MESH)
 
     barrier = pltpu.get_barrier_semaphore()
+    pl.semaphore_signal(barrier, inc=1, device_id={"groups": 1 - mg}, device_id_type=MESH)
     for r in range(1, n):
         pl.semaphore_signal(barrier, inc=1, device_id={"img": img_peer(r)}, device_id_type=MESH)
     for r in range(1, ns):
         pl.semaphore_signal(barrier, inc=1, device_id=samp_peer(r)[1], device_id_type=MESH)
+    small = [pltpu.make_async_copy(a, b, small_sem.at[i]) for i, (a, b) in enumerate(
+        ((order_hbm, order), (noise_hbm, noise), (norm_hbm, norm)))]
+    for copy in small:
+        copy.start()
     for c in range(nc):
         own_copy(c).start()
         for p in range(2):
             image_copy(c, p).start()
-    pl.semaphore_wait(barrier, n - 1 + ns - 1)
+    pl.semaphore_wait(barrier, n + ns - 1)
     for c in range(nc):
         for r in range(1, n):
             gather_copy(c, r, me).start()
 
-    perm = (lax.broadcasted_iota(jnp.int32, (orient, orient), 1) == order[...]).astype(F32).astype(BF16)
+    for copy in small:
+        copy.wait()
+    perm = (lax.broadcasted_iota(jnp.int32, (orient, orient), 0) == order[...]).astype(F32)
+    perm = perm.T.astype(BF16)
+
+    def forward(c):
+        for r in range(1, n):
+            gather_copy(c, r, lax.rem(me + n - r, n)).wait_recv()
+            forward_copy(c, r, mg).start()
+
+    forward(0)
 
     def score_step(c, carry):
         total, power = carry
+
+        @pl.when(c + 1 < nc)
+        def _():
+            forward(c + 1)
+
         own_copy(c).wait()
         for p in range(2):
             image_copy(c, p).wait()
         for r in range(1, n):
-            gather_copy(c, r, lax.rem(me + n - r, n)).wait_recv()
+            forward_copy(c, r, 1 - mg).wait_recv()
         weight = noise[:, cols(c)]
         for p in range(2):
-            block = gat[c, :, p].astype(F32).reshape(orient, ch).astype(BF16)
+            block = gat[c, p].astype(F32).reshape(orient, ch).astype(BF16)
             refs = jnp.dot(perm, block, preferred_element_type=F32)
             scaled = refs * weight
             power = power + jnp.sum(refs * scaled, axis=1, keepdims=True)
@@ -140,6 +167,7 @@
     def drain(c, _):
         for r in range(1, n):
             gather_copy(c, r, me).wait_send()
+            forward_copy(c, r, mg).wait_send()
             sum_copy(c, r).wait_send()
         return 0
 
@@ -160,21 +188,27 @@
     out = pl.pallas_call(
         functools.partial(kernel, n, nx, nc, scale),
         out_shape=jax.ShapeDtypeStruct((2, rows, samples), BF16),
-        in_specs=[hbm, hbm, vmem, vmem, vmem],
+        in_specs=[hbm] * 5,
         out_specs=vmem,
         scratch_shapes=[
+            pltpu.VMEM((1, samples), F32),
+            pltpu.VMEM((1, count), F32),
+            pltpu.VMEM((1, orient), jnp.int32),
             pltpu.VMEM((nc, 2, count, ch), BF16),
-            pltpu.VMEM((nc, n, 2, rows, ch), BF16),
+            pltpu.VMEM((nc, 2, n, rows, ch), BF16),
             pltpu.VMEM((ns, orient // ns, count), F32),
             pltpu.VMEM((ns - 1, orient // ns, count), F32),
             pltpu.VMEM((ns, orient // ns, count), BF16),
             pltpu.VMEM((nc, n, 2, rows, ch), BF16),
             pltpu.VMEM((nc, n - 1, 2, rows, ch), BF16),
             pltpu.VMEM((nc, n, 2, rows, ch), F32),
+            dma((3,)),
             dma((nc, 2)),
             dma((nc,)),
             dma((nc, n - 1)),
             dma((nc, n - 1)),
+            dma((nc, n - 1)),
+            dma((nc, n - 1)),
             dma((ns - 1,)),
             dma((ns - 1,)),
             dma((ns - 1,)),
@@ -183,12 +217,12 @@
             dma((nc, n - 1)),
         ],
         compiler_params=pltpu.CompilerParams(
-            collective_id=0, has_side_effects=True, vmem_limit_bytes=48 * 1024 * 1024),
+            collective_id=0, has_side_effects=True, vmem_limit_bytes=63 * 1024 * 1024),
         cost_estimate=pl.CostEstimate(
             flops=8 * orient * count * samples, bytes_accessed=4 * count * samples,
             transcendentals=orient * count),
     )(references, images, noise_weight.reshape(1, samples), normalizer.reshape(1, count),
-      owner_order.reshape(orient, 1))
+      owner_order.reshape(1, orient))
     return jnp.transpose(out, (1, 0, 2))
 
 

time: 41.9 us -> 40.4 us (0.964)
  local copies, waits for them, and re-layouts: 3.83 us -> 1.7 us
  Pallas kernels: 37.8 us -> 38.6 us
    unnamed x6 -> x0, local copies, waits for them, and re-layouts: 2.3 us -> none
    transpose x1, local copies, waits for them, and re-layouts: 0.79 us -> 1.7 us  [local(): return jnp.transpose(out, (1, 0, 2))]
    pallas_call x1, Pallas kernels: 37.8 us -> 38.6 us  [local(): pl.pallas_call(functools.partial(kernel, n, nx, nc, scale), out_shape=jax...]
    reshape x1 -> x0, local copies, waits for them, and re-layouts: 0.74 us -> none  [local(): owner_order.reshape(orient, 1)]
where the time goes in v2:
time: 40.4 us; the launch traced here: 40.3 us
  Pallas kernels  38.6 us (96%)
  local copies, waits for them, and re-layouts  1.7 us (4%)
    pallas_call x1, Pallas kernels, local(): pl.pallas_call(functools.partial(kernel, n, nx, nc, scale), out_shape=jax...  38.6 us
    transpose x1, local copies, waits for them, and re-layouts, local(): return jnp.transpose(out, (1, 0, 2))  1.7 us

profile of v2, /device:TPU:0, one launch (start us, length us, event | category | flops | bytes accessed | tf_op | source)
XLA Modules:
  0.0 40.3 jit_solution(9150901820635186849)
XLA Ops:
  0.0 38.6 %shard_map.55 = bf16[2,8,4096]{2,1,0:T(8,128)(2,1)} custom-call(bf16[2,8,4096]{2,1,0:T(8,128)(2,1)} %refs_hbm.1, bf16[2,512,4096]{2,1,0:T(8,128)(2,1)} %images_hbm.1, f32[1,4096]{1,0:T(1,128)} %bitcast.5, f32[1,512]{1,0:T(1,128)} %bitcast.6, s32[1,32]{1,0:T(1,128)} %bitcast.7), custom_call_target="tpu_custom_call" | custom-call | flops 536870912 | bytes 8388608 | tf_op jit(solution)/shard_map/pallas_call | solution.py:188
  38.6 1.7 %copy.6 = bf16[8,2,4096]{2,1,0:T(2,128)(2,1)} copy(bf16[8,2,4096]{2,0,1:T(8,128)(2,1)} %bitcast.4) | data formatting | bytes 262144 | tf_op jit(solution)/shard_map/transpose | solution.py:226

commit v3 on v2

--- a/solution.py
+++ b/solution.py
@@ -139,26 +139,112 @@
         post_copy(r, lax.rem(ms + ns - r, ns)).wait_recv()
     weights = post[...].astype(F32).reshape(orient, count).astype(BF16)
 
-    def sum_step(c, _):
+    def local_sums(c):
         for p in range(2):
-            sums = jnp.dot(weights, img_v[c, p], preferred_element_type=F32).reshape(n, rows, ch)
-            own[c, :, p] = sums
-            sbuf[c, :, p] = sums.astype(BF16)
-        for r in range(1, n):
-            sum_copy(c, r).start()
-        return 0
-
-    lax.fori_loop(0, nc, sum_step, 0)
-
-    def out_step(c, _):
-        value = own[c, me]
-        for r in range(1, n):
-            sum_copy(c, r).wait_recv()
-            value = value + rbuf[c, r - 1].astype(F32)
+            own[c, :, p] = jnp.dot(
+                weights, img_v[c, p], preferred_element_type=F32).reshape(n, rows, ch)
+
+    def emit(c, value):
         out[:, :, cols(c)] = (value * scale).astype(BF16)
-        return 0
-
-    lax.fori_loop(0, nc, out_step, 0)
+
+    if n == 4:
+        end = jnp.logical_or(me == 0, me == 3)
+        low = me < 2
+        other = 3 - me
+        near = lax.select(end, lax.select(low, 1, 2), lax.select(low, 0, 3))
+        far = 3 - near
+
+        def hop(c, block, slot, to):
+            return pltpu.make_async_remote_copy(
+                sbuf.at[c, block], rbuf.at[c, slot], o_send.at[c, slot], o_recv.at[c, slot],
+                device_id={"img": to}, device_id_type=MESH)
+
+        @pl.when(end)
+        def _():
+            def first(c, _):
+                local_sums(c)
+                sbuf[c] = own[c].astype(BF16)
+                hop(c, other, 0, near).start()
+                return 0
+
+            def second(c, _):
+                hop(c, far, 1, near).start()
+                return 0
+
+            def third(c, _):
+                hop(c, near, 2, near).start()
+                return 0
+
+            def last(c, _):
+                hop(c, other, 0, near).wait_recv()
+                emit(c, own[c, me] + rbuf[c, 0].astype(F32))
+                return 0
+
+            def drained(c, _):
+                hop(c, other, 0, near).wait_send()
+                hop(c, far, 1, near).wait_send()
+                hop(c, near, 2, near).wait_send()
+                return 0
+
+            for step in (first, second, third, last, drained):
+                lax.fori_loop(0, nc, step, 0)
+
+        @pl.when(jnp.logical_not(end))
+        def _():
+            def add(c, block, slot):
+                hop(c, block, slot, other).wait_recv()
+                sbuf[c, block] = (own[c, block] + rbuf[c, slot].astype(F32)).astype(BF16)
+
+            def first(c, _):
+                local_sums(c)
+                add(c, far, 0)
+                hop(c, far, 3, other).start()
+                return 0
+
+            def second(c, _):
+                add(c, near, 3)
+                hop(c, near, 0, near).start()
+                return 0
+
+            def third(c, _):
+                add(c, other, 1)
+                hop(c, other, 4, other).start()
+                return 0
+
+            def last(c, _):
+                hop(c, other, 2, other).wait_recv()
+                hop(c, other, 4, other).wait_recv()
+                emit(c, own[c, me] + rbuf[c, 2].astype(F32) + rbuf[c, 4].astype(F32))
+                return 0
+
+            def drained(c, _):
+                hop(c, far, 3, other).wait_send()
+                hop(c, near, 0, near).wait_send()
+                hop(c, other, 4, other).wait_send()
+                return 0
+
+            for step in (first, second, third, last, drained):
+                lax.fori_loop(0, nc, step, 0)
+    else:
+        def sum_step(c, _):
+            local_sums(c)
+            sbuf[c] = own[c].astype(BF16)
+            for r in range(1, n):
+                sum_copy(c, r).start()
+            return 0
+
+        def out_step(c, _):
+            value = own[c, me]
+            for r in range(1, n):
+                sum_copy(c, r).wait_recv()
+                value = value + rbuf[c, r - 1].astype(F32)
+            emit(c, value)
+            for r in range(1, n):
+                sum_copy(c, r).wait_send()
+            return 0
+
+        lax.fori_loop(0, nc, sum_step, 0)
+        lax.fori_loop(0, nc, out_step, 0)
 
     for r in range(1, ns):
         score_copy(r).wait_send()
@@ -168,7 +254,6 @@
         for r in range(1, n):
             gather_copy(c, r, me).wait_send()
             forward_copy(c, r, mg).wait_send()
-            sum_copy(c, r).wait_send()
         return 0
 
     lax.fori_loop(0, nc, drain, 0)
@@ -181,6 +266,7 @@
     orient = n * rows
     ch = 1024
     nc = samples // ch
+    slots = 5 if n == 4 else n - 1
     scale = 1.0 / (float(count * n) ** 0.5)
     dma = pltpu.SemaphoreType.DMA
     vmem = pl.BlockSpec(memory_space=pltpu.VMEM)
@@ -200,7 +286,7 @@
             pltpu.VMEM((ns - 1, orient // ns, count), F32),
             pltpu.VMEM((ns, orient // ns, count), BF16),
             pltpu.VMEM((nc, n, 2, rows, ch), BF16),
-            pltpu.VMEM((nc, n - 1, 2, rows, ch), BF16),
+            pltpu.VMEM((nc, slots, 2, rows, ch), BF16),
             pltpu.VMEM((nc, n, 2, rows, ch), F32),
             dma((3,)),
             dma((nc, 2)),
@@ -213,8 +299,8 @@
             dma((ns - 1,)),
             dma((ns - 1,)),
             dma((ns - 1,)),
-            dma((nc, n - 1)),
-            dma((nc, n - 1)),
+            dma((nc, slots)),
+            dma((nc, slots)),
         ],
         compiler_params=pltpu.CompilerParams(
             collective_id=0, has_side_effects=True, vmem_limit_bytes=63 * 1024 * 1024),

time: 40.4 us -> 39.9 us (0.988)
  Pallas kernels: 38.6 us -> 38.1 us
    pallas_call x1, Pallas kernels: 38.6 us -> 38.1 us  [local(): pl.pallas_call(functools.partial(kernel, n, nx, nc, scale), out_shape=jax...]
where the time goes in v3:
time: 39.9 us; the launch traced here: 39.8 us
  Pallas kernels  38.1 us (95%)
  local copies, waits for them, and re-layouts  1.7 us (4%)
    pallas_call x1, Pallas kernels, local(): pl.pallas_call(functools.partial(kernel, n, nx, nc, scale), out_shape=jax...  38.1 us
    transpose x1, local copies, waits for them, and re-layouts, local(): return jnp.transpose(out, (1, 0, 2))  1.7 us

profile of v3, /device:TPU:0, one launch (start us, length us, event | category | flops | bytes accessed | tf_op | source)
XLA Modules:
  0.0 39.8 jit_solution(9346415700497668145)
XLA Ops:
  0.0 38.1 %shard_map.55 = bf16[2,8,4096]{2,1,0:T(8,128)(2,1)} custom-call(bf16[2,8,4096]{2,1,0:T(8,128)(2,1)} %refs_hbm.1, bf16[2,512,4096]{2,1,0:T(8,128)(2,1)} %images_hbm.1, f32[1,4096]{1,0:T(1,128)} %bitcast.5, f32[1,512]{1,0:T(1,128)} %bitcast.6, s32[1,32]{1,0:T(1,128)} %bitcast.7), custom_call_target="tpu_custom_call" | custom-call | flops 536870912 | bytes 8388608 | tf_op jit(solution)/shard_map/pallas_call | solution.py:274
  38.1 1.7 %copy.6 = bf16[8,2,4096]{2,1,0:T(2,128)(2,1)} copy(bf16[8,2,4096]{2,0,1:T(8,128)(2,1)} %bitcast.4) | data formatting | bytes 262144 | tf_op jit(solution)/shard_map/transpose | solution.py:312

commit v4 on v3

--- a/solution.py
+++ b/solution.py
@@ -39,17 +39,17 @@
         return pltpu.make_async_copy(images_hbm.at[p, :, cols(c)], img_v.at[c, p], img_sem.at[c, p])
 
     def own_copy(c):
-        return pltpu.make_async_copy(refs_hbm.at[:, :, cols(c)], gat.at[c, :, me], own_sem.at[c])
+        return pltpu.make_async_copy(refs_hbm.at[mg, :, cols(c)], gat.at[c, mg, me], own_sem.at[c])
 
     def gather_copy(c, r, slot):
         return pltpu.make_async_remote_copy(
             refs_hbm.at[mg, :, cols(c)], gat.at[c, mg, slot], g_send.at[c, r - 1], g_recv.at[c, r - 1],
             device_id={"img": img_peer(r)}, device_id_type=MESH)
 
-    def forward_copy(c, r, part):
-        block = gat.at[c, part, lax.rem(me + n - r, n)]
-        return pltpu.make_async_remote_copy(
-            block, block, f_send.at[c, r - 1], f_recv.at[c, r - 1],
+    def forward_copy(c, part):
+        block = gat.at[c, part]
+        return pltpu.make_async_remote_copy(
+            block, block, f_send.at[c], f_recv.at[c],
             device_id={"groups": 1 - mg}, device_id_type=MESH)
 
     def score_copy(r):
@@ -94,45 +94,39 @@
     perm = (lax.broadcasted_iota(jnp.int32, (orient, orient), 0) == order[...]).astype(F32)
     perm = perm.T.astype(BF16)
 
-    def forward(c):
+    def score(c, p, carry):
+        total, power = carry
+        image_copy(c, p).wait()
+        block = gat[c, p].astype(F32).reshape(orient, ch).astype(BF16)
+        refs = jnp.dot(perm, block, preferred_element_type=F32)
+        scaled = refs * noise[:, cols(c)]
+        power = power + jnp.sum(refs * scaled, axis=1, keepdims=True)
+        total = total + lax.dot_general(
+            scaled.astype(BF16), img_v[c, p], (((1,), (1,)), ((), ())), preferred_element_type=F32)
+        return total, power
+
+    def gathered(c, carry):
+        own_copy(c).wait()
         for r in range(1, n):
             gather_copy(c, r, lax.rem(me + n - r, n)).wait_recv()
-            forward_copy(c, r, mg).start()
-
-    forward(0)
-
-    def score_step(c, carry):
-        total, power = carry
-
-        @pl.when(c + 1 < nc)
-        def _():
-            forward(c + 1)
-
-        own_copy(c).wait()
-        for p in range(2):
-            image_copy(c, p).wait()
-        for r in range(1, n):
-            forward_copy(c, r, 1 - mg).wait_recv()
-        weight = noise[:, cols(c)]
-        for p in range(2):
-            block = gat[c, p].astype(F32).reshape(orient, ch).astype(BF16)
-            refs = jnp.dot(perm, block, preferred_element_type=F32)
-            scaled = refs * weight
-            power = power + jnp.sum(refs * scaled, axis=1, keepdims=True)
-            total = total + lax.dot_general(
-                scaled.astype(BF16), img_v[c, p], (((1,), (1,)), ((), ())), preferred_element_type=F32)
-        return total, power
-
-    total, power = lax.fori_loop(
-        0, nc, score_step, (jnp.zeros((orient, count), F32), jnp.zeros((orient, 1), F32)))
+        forward_copy(c, mg).start()
+        return score(c, mg, carry)
+
+    def forwarded(c, carry):
+        forward_copy(c, 1 - mg).wait_recv()
+        return score(c, 1 - mg, carry)
+
+    carry = (jnp.zeros((orient, count), F32), jnp.zeros((orient, 1), F32))
+    carry = lax.fori_loop(0, nc, gathered, carry)
+    total, power = lax.fori_loop(0, nc, forwarded, carry)
     sc_send[...] = (total - 0.5 * power).reshape(sc_send.shape)
     for r in range(1, ns):
         score_copy(r).start()
-    score = sc_send[ms]
+    row = sc_send[ms]
     for r in range(1, ns):
         score_copy(r).wait_recv()
-        score = score + sc_recv[r - 1]
-    post[ms] = jnp.exp(score - norm[...]).astype(BF16)
+        row = row + sc_recv[r - 1]
+    post[ms] = jnp.exp(row - norm[...]).astype(BF16)
     for r in range(1, ns):
         post_copy(r, ms).start()
     for r in range(1, ns):
@@ -253,7 +247,7 @@
     def drain(c, _):
         for r in range(1, n):
             gather_copy(c, r, me).wait_send()
-            forward_copy(c, r, mg).wait_send()
+        forward_copy(c, mg).wait_send()
         return 0
 
     lax.fori_loop(0, nc, drain, 0)
@@ -264,7 +258,7 @@
     _, rows, samples = references.shape
     count = images.shape[1]
     orient = n * rows
-    ch = 1024
+    ch = min(1024, samples)
     nc = samples // ch
     slots = 5 if n == 4 else n - 1
     scale = 1.0 / (float(count * n) ** 0.5)
@@ -293,8 +287,8 @@
             dma((nc,)),
             dma((nc, n - 1)),
             dma((nc, n - 1)),
-            dma((nc, n - 1)),
-            dma((nc, n - 1)),
+            dma((nc,)),
+            dma((nc,)),
             dma((ns - 1,)),
             dma((ns - 1,)),
             dma((ns - 1,)),

time: 39.9 us -> 37.4 us (0.937)
  Pallas kernels: 38.1 us -> 35.5 us
    pallas_call x1, Pallas kernels: 38.1 us -> 35.5 us  [local(): pl.pallas_call(functools.partial(kernel, n, nx, nc, scale), out_shape=jax...]
where the time goes in v4:
time: 37.4 us; the launch traced here: 37.2 us
  Pallas kernels  35.5 us (95%)
  local copies, waits for them, and re-layouts  1.7 us (5%)
    pallas_call x1, Pallas kernels, local(): pl.pallas_call(functools.partial(kernel, n, nx, nc, scale), out_shape=jax...  35.5 us
    transpose x1, local copies, waits for them, and re-layouts, local(): return jnp.transpose(out, (1, 0, 2))  1.7 us

profile of v4, /device:TPU:0, one launch (start us, length us, event | category | flops | bytes accessed | tf_op | source)
XLA Modules:
  0.0 37.2 jit_solution(16786035211997997889)
XLA Ops:
  0.0 35.5 %shard_map.55 = bf16[2,8,4096]{2,1,0:T(8,128)(2,1)} custom-call(bf16[2,8,4096]{2,1,0:T(8,128)(2,1)} %refs_hbm.1, bf16[2,512,4096]{2,1,0:T(8,128)(2,1)} %images_hbm.1, f32[1,4096]{1,0:T(1,128)} %bitcast.5, f32[1,512]{1,0:T(1,128)} %bitcast.6, s32[1,32]{1,0:T(1,128)} %bitcast.7), custom_call_target="tpu_custom_call" | custom-call | flops 536870912 | bytes 8388608 | tf_op jit(solution)/shard_map/pallas_call | solution.py:268
  35.5 1.7 %copy.6 = bf16[8,2,4096]{2,1,0:T(2,128)(2,1)} copy(bf16[8,2,4096]{2,0,1:T(8,128)(2,1)} %bitcast.4) | data formatting | bytes 262144 | tf_op jit(solution)/shard_map/transpose | solution.py:306

commit v5 on v4

--- a/solution.py
+++ b/solution.py
@@ -12,8 +12,8 @@
 
 
 def kernel(n, nx, nc, scale, refs_hbm, images_hbm, noise_hbm, norm_hbm, order_hbm, out,
-           noise, norm, order, img_v, gat, sc_send, sc_recv, post, sbuf, rbuf, own,
-           small_sem, img_sem, own_sem, g_send, g_recv, f_send, f_recv, s_send, s_recv, p_send, p_recv, o_send, o_recv):
+           noise, norm, order, img_v, gat, parts, sbuf, rbuf, own,
+           small_sem, img_sem, own_sem, g_send, g_recv, f_send, f_recv, s_send, s_recv, o_send, o_recv):
     ns = 2 * nx
     rows = refs_hbm.shape[1]
     orient = n * rows
@@ -33,7 +33,7 @@
 
     def samp_peer(r):
         t = lax.rem(ms + r, ns)
-        return t, {"samp": t // 2, "sub": lax.rem(t, 2)}
+        return {"samp": t // 2, "sub": lax.rem(t, 2)}
 
     def image_copy(c, p):
         return pltpu.make_async_copy(images_hbm.at[p, :, cols(c)], img_v.at[c, p], img_sem.at[c, p])
@@ -52,17 +52,10 @@
             block, block, f_send.at[c], f_recv.at[c],
             device_id={"groups": 1 - mg}, device_id_type=MESH)
 
-    def score_copy(r):
-        t, dev = samp_peer(r)
+    def score_copy(r, slot):
         return pltpu.make_async_remote_copy(
-            sc_send.at[t], sc_recv.at[r - 1], s_send.at[r - 1], s_recv.at[r - 1],
-            device_id=dev, device_id_type=MESH)
-
-    def post_copy(r, slot):
-        _, dev = samp_peer(r)
-        return pltpu.make_async_remote_copy(
-            post.at[slot], post.at[slot], p_send.at[r - 1], p_recv.at[r - 1],
-            device_id=dev, device_id_type=MESH)
+            parts.at[slot], parts.at[slot], s_send.at[r - 1], s_recv.at[r - 1],
+            device_id=samp_peer(r), device_id_type=MESH)
 
     def sum_copy(c, r):
         d = img_peer(r)
@@ -75,7 +68,7 @@
     for r in range(1, n):
         pl.semaphore_signal(barrier, inc=1, device_id={"img": img_peer(r)}, device_id_type=MESH)
     for r in range(1, ns):
-        pl.semaphore_signal(barrier, inc=1, device_id=samp_peer(r)[1], device_id_type=MESH)
+        pl.semaphore_signal(barrier, inc=1, device_id=samp_peer(r), device_id_type=MESH)
     small = [pltpu.make_async_copy(a, b, small_sem.at[i]) for i, (a, b) in enumerate(
         ((order_hbm, order), (noise_hbm, noise), (norm_hbm, norm)))]
     for copy in small:
@@ -119,19 +112,15 @@
     carry = (jnp.zeros((orient, count), F32), jnp.zeros((orient, 1), F32))
     carry = lax.fori_loop(0, nc, gathered, carry)
     total, power = lax.fori_loop(0, nc, forwarded, carry)
-    sc_send[...] = (total - 0.5 * power).reshape(sc_send.shape)
+    parts[ms] = total - 0.5 * power
     for r in range(1, ns):
-        score_copy(r).start()
-    row = sc_send[ms]
+        score_copy(r, ms).start()
     for r in range(1, ns):
-        score_copy(r).wait_recv()
-        row = row + sc_recv[r - 1]
-    post[ms] = jnp.exp(row - norm[...]).astype(BF16)
-    for r in range(1, ns):
-        post_copy(r, ms).start()
-    for r in range(1, ns):
-        post_copy(r, lax.rem(ms + ns - r, ns)).wait_recv()
-    weights = post[...].astype(F32).reshape(orient, count).astype(BF16)
+        score_copy(r, lax.rem(ms + ns - r, ns)).wait_recv()
+    scores = parts[0]
+    for i in range(1, ns):
+        scores = scores + parts[i]
+    weights = jnp.exp(scores - norm[...]).astype(BF16)
 
     def local_sums(c):
         for p in range(2):
@@ -241,8 +230,7 @@
         lax.fori_loop(0, nc, out_step, 0)
 
     for r in range(1, ns):
-        score_copy(r).wait_send()
-        post_copy(r, ms).wait_send()
+        score_copy(r, ms).wait_send()
 
     def drain(c, _):
         for r in range(1, n):
@@ -276,9 +264,7 @@
             pltpu.VMEM((1, orient), jnp.int32),
             pltpu.VMEM((nc, 2, count, ch), BF16),
             pltpu.VMEM((nc, 2, n, rows, ch), BF16),
-            pltpu.VMEM((ns, orient // ns, count), F32),
-            pltpu.VMEM((ns - 1, orient // ns, count), F32),
-            pltpu.VMEM((ns, orient // ns, count), BF16),
+            pltpu.VMEM((ns, orient, count), F32),
             pltpu.VMEM((nc, n, 2, rows, ch), BF16),
             pltpu.VMEM((nc, slots, 2, rows, ch), BF16),
             pltpu.VMEM((nc, n, 2, rows, ch), F32),
@@ -289,8 +275,6 @@
             dma((nc, n - 1)),
             dma((nc,)),
             dma((nc,)),
-            dma((ns - 1,)),
-            dma((ns - 1,)),
             dma((ns - 1,)),
             dma((ns - 1,)),
             dma((nc, slots)),

time: 37.4 us -> 35.7 us (0.955)
  Pallas kernels: 35.5 us -> 33.9 us
    pallas_call x1, Pallas kernels: 35.5 us -> 33.9 us  [local(): pl.pallas_call(functools.partial(kernel, n, nx, nc, scale), out_shape=jax...]
where the time goes in v5:
time: 35.7 us; the launch traced here: 35.6 us
  Pallas kernels  33.9 us (95%)
  local copies, waits for them, and re-layouts  1.7 us (5%)
    pallas_call x1, Pallas kernels, local(): pl.pallas_call(functools.partial(kernel, n, nx, nc, scale), out_shape=jax...  33.9 us
    transpose x1, local copies, waits for them, and re-layouts, local(): return jnp.transpose(out, (1, 0, 2))  1.7 us

profile of v5, /device:TPU:0, one launch (start us, length us, event | category | flops | bytes accessed | tf_op | source)
XLA Modules:
  0.0 35.6 jit_solution(8173644186749805192)
XLA Ops:
  0.0 33.9 %shard_map.55 = bf16[2,8,4096]{2,1,0:T(8,128)(2,1)} custom-call(bf16[2,8,4096]{2,1,0:T(8,128)(2,1)} %refs_hbm.1, bf16[2,512,4096]{2,1,0:T(8,128)(2,1)} %images_hbm.1, f32[1,4096]{1,0:T(1,128)} %bitcast.5, f32[1,512]{1,0:T(1,128)} %bitcast.6, s32[1,32]{1,0:T(1,128)} %bitcast.7), custom_call_target="tpu_custom_call" | custom-call | flops 536870912 | bytes 8388608 | tf_op jit(solution)/shard_map/pallas_call | solution.py:256
  33.9 1.7 %copy.6 = bf16[8,2,4096]{2,1,0:T(2,128)(2,1)} copy(bf16[8,2,4096]{2,0,1:T(8,128)(2,1)} %bitcast.4) | data formatting | bytes 262144 | tf_op jit(solution)/shard_map/transpose | solution.py:290
